TPU v7x, 128 devices: a whole 4x4x4 slice. The times are simulated.
128 devices in a mesh: rows: 32 (over z, y, core), cols: 4 (over x).
Axes of the slice: x: 4, y: 4, z: 4, core: 2. Of those that a mesh axis runs over, the one named last changes fastest.
Arguments:
- snapshots: float32 [65536, 4096], P('rows', 'cols'), may hold values from -27 to 27
Outputs:
- r_factor: float32 [128, 128], replicated
- coupling: float32 [128, 4096], P(None, 'cols')
- updated: float32 [65536, 4096], P('rows', 'cols')
All inputs are finite; a program needn't handle non-finite values.
Results may differ from a plain program's by a relative error of at most 0.00025.
Values sent between devices are 32-bit elements; how exact they have to be, the bound alone decides.
A program may use at most 64 MiB of HBM per device.

v0:
```python
import jax
import jax.numpy as jnp
from jax import lax
from jax.experimental import pallas as pl
from jax.experimental.pallas import tpu as pltpu
from jax.sharding import PartitionSpec as P

MESH = pl.DeviceIdType.MESH
F32 = jnp.float32
BF16 = jnp.bfloat16
PANEL = 128
ROWS = 2048
COLS = 1024
HALF = COLS // 2
CHIPS = 16
BLOCK = 256
BLOCKS = ROWS // BLOCK
CHUNK = 64
CHUNKS = ROWS // CHUNK
SIDE = CHUNKS // 2
DIRECT = 3
PER = BLOCK // CHUNK
PIECE = PANEL // CHIPS
TILE = 512
GROUP = 16
SIZE = 4
UNIT = 128
UNITS = ROWS // UNIT
NEAR = sorted(
    ((dz, dy) for dz in range(SIZE) for dy in range(SIZE) if dz or dy),
    key=lambda at: min(at[0], SIZE - at[0]) + min(at[1], SIZE - at[1]),
)
FAR = NEAR[::-1]


def slot(at):
    return at[0] * SIZE + at[1]


def split(value):
    high = value.astype(BF16)
    low = (value - high.astype(F32)).astype(BF16)
    return high, low


def cross(left, right):
    return lax.dot_general(left, right, (((0,), (0,)), ((), ())), preferred_element_type=F32)


def plain(left, right):
    return lax.dot_general(left, right, (((1,), (0,)), ((), ())), preferred_element_type=F32)


def inverse(value):
    guess = pl.reciprocal(value, approx=True)
    return guess * (2.0 - value * guess)


def triple(value):
    one = value.astype(BF16)
    rest = value - one.astype(F32)
    two = rest.astype(BF16)
    return one, two, (rest - two.astype(F32)).astype(BF16)


def cholesky(gram_ref, packed_ref):
    shape = (GROUP, PANEL)
    sub = lax.broadcasted_iota(jnp.int32, shape, 0)
    lane = lax.broadcasted_iota(jnp.int32, shape, 1)

    def across(value, k):
        return jnp.broadcast_to(value[k : k + 1, :], shape)

    count = PANEL // GROUP
    lefts = [gram_ref[n * GROUP : (n + 1) * GROUP, :] for n in range(count)]
    rights = [(lane == sub + n * GROUP).astype(F32) for n in range(count)]
    for n in range(count):
        base = n * GROUP
        top, side = lefts[n], rights[n]
        columns = [jnp.broadcast_to(top[:, base + k : base + k + 1], shape) for k in range(GROUP)]
        pivot = across(columns[0], 0)
        pivots = pivot
        for k in range(GROUP - 1):
            recip = inverse(pivot)
            link = across(columns[k + 1], k)
            pivot = across(columns[k + 1], k + 1) - (link * recip) * link
            pivots = jnp.where(sub > k, pivot, pivots)
            factor = jnp.where(sub > k, columns[k] * recip, 0.0)
            for j in range(k + 1, GROUP):
                columns[j] = columns[j] - factor * across(columns[j], k)
            top, side = top - factor * across(top, k), side - factor * across(side, k)
        scale = lax.rsqrt(pivots)
        scale = scale * (1.5 - 0.5 * pivots * scale * scale)
        top = jnp.where(lane >= sub + base, top * scale, 0.0)
        side = side * scale
        packed_ref[base : base + GROUP, :] = jnp.where(lane >= sub + base, top, side)
        if n + 1 < count:
            one, two, three = triple(jnp.concatenate([top, side], axis=1))
            update = cross(
                jnp.concatenate([v[:, :PANEL] for v in (one, one, two, two, one, three)], axis=0),
                jnp.concatenate([one, two, one, two, three, one], axis=0),
            )
            for m in range(n + 1, count):
                rows = update[m * GROUP : (m + 1) * GROUP]
                lefts[m] = lefts[m] - rows[:, :PANEL]
                rights[m] = rights[m] - rows[:, PANEL:]


def gather_kernel(
    snap, kept, panel2, total, packed,
    pbuf, high, low, wacc, swap, mine, parts, gram, gparts, gsum, gswap, gfull,
    load_sem, pload_sem, bs_send, bs_recv, ex_send, ex_recv, rs_send, rs_recv, ag_send, ag_recv,
    fx_send, fx_recv, gr_send, gr_recv, gx_send, gx_recv, ga_send, ga_recv, u_send, u_recv, meet,
):
    row = lax.axis_index("rows")
    col = lax.axis_index("cols")
    chip = row // 2
    core = row % 2
    partner = (chip * 2 + 1 - core, col)
    high_axis, low_axis = chip // SIZE, chip % SIZE

    def away(at):
        return ((high_axis + at[0]) % SIZE) * SIZE + (low_axis + at[1]) % SIZE

    def peer(at):
        return away(at) * 2 + core

    along_x = [(row, (col + step) % SIZE) for step in (1, SIZE - 1)]
    along_low = [(peer((0, step)), col) for step in (1, SIZE - 1)]
    along_high = [(peer((step, 0)), col) for step in (1, SIZE - 1)]
    rounds = [along_x + along_low, along_high, along_high]

    def announce(index):
        for other in rounds[index]:
            pl.semaphore_signal(meet.at[index], inc=1, device_id=other, device_id_type=MESH)

    def await_round(index):
        pl.semaphore_wait(meet.at[index], len(rounds[index]))

    greeted = along_x + along_low + along_high + [partner]
    barrier = pltpu.get_barrier_semaphore()
    for other in greeted:
        pl.semaphore_signal(barrier, inc=1, device_id=other, device_id_type=MESH)

    def load(block):
        rows = pl.ds(pl.multiple_of(block * BLOCK, BLOCK), BLOCK)
        return pltpu.make_async_copy(snap.at[rows], kept.at[rows], load_sem.at[block])

    panel_load = pltpu.make_async_copy(snap.at[:, pl.ds(0, PANEL)], pbuf, pload_sem)

    @pl.when(col == 0)
    def _():
        panel_load.start()

    def start_load(block, carry):
        load(block).start()
        return carry

    @pl.when(col != 0)
    def _():
        lax.fori_loop(0, BLOCKS, start_load, 0)

    pl.semaphore_wait(barrier, len(greeted))

    def chunk_rows(chunk):
        return pl.ds(pl.multiple_of(chunk * CHUNK, CHUNK), CHUNK)

    def relay(chunk, target):
        rows = chunk_rows(chunk)
        return pltpu.make_async_remote_copy(
            src_ref=pbuf.at[rows], dst_ref=pbuf.at[rows], send_sem=bs_send.at[chunk],
            recv_sem=bs_recv.at[chunk], device_id=(row, target), device_id_type=MESH,
        )

    def first(chunk, target, extra=0):
        rows = chunk_rows(chunk)
        return pltpu.make_async_remote_copy(
            src_ref=snap.at[rows, pl.ds(0, PANEL)], dst_ref=pbuf.at[rows], send_sem=bs_send.at[chunk + extra],
            recv_sem=bs_recv.at[chunk], device_id=(row, target), device_id_type=MESH,
        )

    @pl.when(col == 0)
    def _():
        def send(step, carry):
            first(step, 1).start()
            first(step + SIDE, 3).start()
            return carry

        def send_direct(step, carry):
            first(step + SIDE, 1, CHUNKS).start()
            first(step, 3, CHUNKS).start()
            return carry

        lax.fori_loop(0, SIDE, send, 0)
        lax.fori_loop(SIDE - DIRECT, SIDE, send_direct, 0)
        lax.fori_loop(0, BLOCKS, start_load, 0)
        announce(0)

    def block_rows(block):
        return pl.ds(pl.multiple_of(block * BLOCK, BLOCK), BLOCK)

    def widen(start, size):
        rows = pl.ds(pl.multiple_of(start, size), size)
        ph, plo = split(pbuf[rows])
        panel2[rows, :PANEL] = ph
        panel2[rows, PANEL:] = plo

    def prepare(block, carry):
        load(block).wait()
        rows = block_rows(block)
        sh, sl = split(kept[rows])
        high[rows] = sh
        low[rows] = sl
        return carry

    def accumulate(start, size):
        rows = pl.ds(pl.multiple_of(start, size), size)
        both = panel2[rows]
        for n in range(COLS // 256):
            columns = pl.ds(n * 256, 256)
            one = cross(both, high[rows, columns])
            two = cross(both[:, :PANEL], low[rows, columns])
            wacc[:, columns] += one[:PANEL] + one[PANEL:] + two

    def gram_piece(step):
        other = away(step)
        return pltpu.make_async_remote_copy(
            src_ref=gram.at[pl.ds(pl.multiple_of(other * PIECE, PIECE), PIECE)], dst_ref=gparts.at[chip],
            send_sem=gr_send.at[slot(step)], recv_sem=gr_recv.at[chip], device_id=(peer(step), col), device_id_type=MESH,
        )

    def gram_arrived(step):
        other = away(step)
        return pltpu.make_async_remote_copy(
            src_ref=gram.at[pl.ds(0, PIECE)], dst_ref=gparts.at[other],
            send_sem=gr_send.at[slot(step)], recv_sem=gr_recv.at[other], device_id=(peer(step), col), device_id_type=MESH,
        )

    @pl.when(col == 0)
    def _():
        panel_load.wait()

        def one(block, carry):
            widen(block * BLOCK, BLOCK)
            return carry

        lax.fori_loop(0, BLOCKS, one, 0)
        full = cross(panel2[...], panel2[...])
        gram[...] = full[:PANEL, :PANEL] + (full[:PANEL, PANEL:] + full[PANEL:, :PANEL]) + full[PANEL:, PANEL:]

        await_round(0)
        announce(1)
        await_round(1)
        announce(2)
        await_round(2)
        for at in FAR:
            gram_piece(at).start()
        gparts[chip] = gram[pl.ds(pl.multiple_of(chip * PIECE, PIECE), PIECE)]

    wacc[...] = jnp.zeros_like(wacc)

    @pl.when(col == 0)
    def _():
        lax.fori_loop(0, BLOCKS, prepare, 0)

        def one(block, carry):
            accumulate(block * BLOCK, BLOCK)
            return carry

        lax.fori_loop(0, BLOCKS, one, 0)

    @pl.when(col != 0)
    def _():
        def pass_on(step):
            straight = (step + jnp.where(col == 3, SIDE, 0)) % CHUNKS
            chunk = jnp.where(col == 2, (step % 2) * SIDE + step // 2, straight)
            onward = jnp.where(chunk < SIDE, col + 1, col - 1)
            relay(chunk, 0).wait_recv()

            @pl.when((onward > 0) & (onward < 4) & ((col != 2) | (chunk % SIDE < SIDE - DIRECT)))
            def _():
                relay(chunk, onward).start()

        def work(index):
            straight = (index + jnp.where(col == 3, UNITS // 2, 0)) % UNITS
            unit = jnp.where(col == 2, (index % 2) * (UNITS // 2) + index // 2, straight)
            widen(unit * UNIT, UNIT)
            accumulate(unit * UNIT, UNIT)

        def early(step, carry):
            pass_on(step)
            prepare(step, 0)
            return carry

        def middle(step, carry):
            pass_on(step)
            work(step - BLOCKS)
            return carry

        def late(pair, carry):
            pass_on(2 * pair)
            work(pair - 1)
            pass_on(2 * pair + 1)
            return carry

        announce(0)
        lax.fori_loop(0, 2, early, 0)
        await_round(0)
        announce(1)
        lax.fori_loop(2, 4, early, 0)
        await_round(1)
        announce(2)
        lax.fori_loop(4, 6, early, 0)
        await_round(2)
        lax.fori_loop(6, BLOCKS, early, 0)
        lax.fori_loop(BLOCKS, 15, middle, 0)
        pass_on(15)
        lax.fori_loop(8, UNITS, late, 0)
        work(UNITS - 1)

    exchange = pltpu.make_async_remote_copy(
        src_ref=wacc.at[:, pl.ds(pl.multiple_of((1 - core) * HALF, HALF), HALF)], dst_ref=swap,
        send_sem=ex_send, recv_sem=ex_recv, device_id=partner, device_id_type=MESH,
    )
    exchange.start()

    gram_swap = pltpu.make_async_remote_copy(
        src_ref=gsum, dst_ref=gswap, send_sem=gx_send, recv_sem=gx_recv, device_id=partner, device_id_type=MESH,
    )

    def gram_gather(step):
        rows = pl.ds(pl.multiple_of(chip * PIECE, PIECE), PIECE)
        return pltpu.make_async_remote_copy(
            src_ref=gfull.at[rows], dst_ref=gfull.at[rows],
            send_sem=ga_send.at[slot(step)], recv_sem=ga_recv.at[chip], device_id=(peer(step), col), device_id_type=MESH,
        )

    def gram_gathered(step):
        other = away(step)
        rows = pl.ds(pl.multiple_of(other * PIECE, PIECE), PIECE)
        return pltpu.make_async_remote_copy(
            src_ref=gfull.at[rows], dst_ref=gfull.at[rows],
            send_sem=ga_send.at[slot(step)], recv_sem=ga_recv.at[other], device_id=(peer(step), col), device_id_type=MESH,
        )

    @pl.when(col == 0)
    def _():
        for at in NEAR:
            gram_arrived(at).wait_recv()
        gsum[...] = jnp.sum(gparts[...], axis=0)
        gram_swap.start()
        gram_swap.wait()
        gfull[pl.ds(pl.multiple_of(chip * PIECE, PIECE), PIECE)] = gsum[...] + gswap[...]

        for at in FAR:
            gram_gather(at).start()

    exchange.wait()
    mine[...] = wacc[:, pl.ds(pl.multiple_of(core * HALF, HALF), HALF)] + swap[...]

    def scatter(step):
        other = away(step)
        return pltpu.make_async_remote_copy(
            src_ref=mine.at[pl.ds(pl.multiple_of(other * PIECE, PIECE), PIECE)], dst_ref=parts.at[chip],
            send_sem=rs_send.at[slot(step)], recv_sem=rs_recv.at[chip], device_id=(peer(step), col), device_id_type=MESH,
        )

    def scattered(step):
        other = away(step)
        return pltpu.make_async_remote_copy(
            src_ref=mine.at[pl.ds(0, PIECE)], dst_ref=parts.at[other],
            send_sem=rs_send.at[slot(step)], recv_sem=rs_recv.at[other], device_id=(peer(step), col), device_id_type=MESH,
        )

    for at in FAR:
        scatter(at).start()
    parts[chip] = mine[pl.ds(pl.multiple_of(chip * PIECE, PIECE), PIECE)]

    def send_packed(target):
        return pltpu.make_async_remote_copy(
            src_ref=packed, dst_ref=packed, send_sem=u_send.at[target], recv_sem=u_recv,
            device_id=(row, target), device_id_type=MESH,
        )

    @pl.when(col == 0)
    def _():
        for at in NEAR:
            gram_gathered(at).wait_recv()
        cholesky(gfull, packed)
        for target in (2, 1, 3):
            send_packed(target).start()

    for at in NEAR:
        scattered(at).wait_recv()
    half = pl.ds(pl.multiple_of(core * HALF, HALF), HALF)
    own = pl.ds(pl.multiple_of(chip * PIECE, PIECE), PIECE)
    total[own, half] = jnp.sum(parts[...], axis=0)

    def gather(step):
        return pltpu.make_async_remote_copy(
            src_ref=total.at[own, half], dst_ref=total.at[own, half],
            send_sem=ag_send.at[slot(step)], recv_sem=ag_recv.at[chip], device_id=(peer(step), col), device_id_type=MESH,
        )

    def gathered(step):
        other = away(step)
        rows = pl.ds(pl.multiple_of(other * PIECE, PIECE), PIECE)
        return pltpu.make_async_remote_copy(
            src_ref=total.at[rows, half], dst_ref=total.at[rows, half],
            send_sem=ag_send.at[slot(step)], recv_sem=ag_recv.at[other], device_id=(peer(step), col), device_id_type=MESH,
        )

    def onward(owner, columns):
        rows = pl.ds(pl.multiple_of(owner * PIECE, PIECE), PIECE)
        return pltpu.make_async_remote_copy(
            src_ref=total.at[rows, columns], dst_ref=total.at[rows, columns], send_sem=fx_send.at[owner],
            recv_sem=fx_recv.at[owner], device_id=partner, device_id_type=MESH,
        )

    for at in FAR:
        gather(at).start()
    onward(chip, half).start()
    for at in NEAR:
        gathered(at).wait_recv()
        onward(away(at), half).start()
    other_half = pl.ds(pl.multiple_of((1 - core) * HALF, HALF), HALF)

    for at in NEAR:
        scatter(at).wait_send()
        gather(at).wait_send()

    @pl.when(col == 0)
    def _():
        for at in NEAR:
            gram_piece(at).wait_send()
            gram_gather(at).wait_send()
        for target in (2, 1, 3):
            send_packed(target).wait_send()

        def sent(chunk, carry):
            first(chunk, 1).wait_send()
            return carry

        lax.fori_loop(0, CHUNKS, sent, 0)

        def sent_direct(step, carry):
            first(step + SIDE, 1, CHUNKS).wait_send()
            first(step, 3, CHUNKS).wait_send()
            return carry

        lax.fori_loop(SIDE - DIRECT, SIDE, sent_direct, 0)

    def sent_on(chunk, carry):
        relay(chunk, 0).wait_send()
        return carry

    @pl.when(col == 1)
    def _():
        lax.fori_loop(0, SIDE, sent_on, 0)

    @pl.when(col == 2)
    def _():
        lax.fori_loop(0, SIDE - DIRECT, sent_on, 0)
        lax.fori_loop(SIDE, CHUNKS - DIRECT, sent_on, 0)

    @pl.when(col == 3)
    def _():
        lax.fori_loop(SIDE, CHUNKS, sent_on, 0)

    @pl.when(col != 0)
    def _():
        send_packed(0).wait_recv()

    def finish(owner, carry):
        onward(owner, half).wait_send()
        onward(owner, other_half).wait_recv()
        return carry

    lax.fori_loop(0, CHIPS, finish, 0)


def apply_kernel(kept, panel2, total, packed, factor, coupling, updated, out, x2, sems):
    both = packed[...]
    sub = lax.broadcasted_iota(jnp.int32, (PANEL, PANEL), 0)
    lane = lax.broadcasted_iota(jnp.int32, (PANEL, PANEL), 1)
    factor[...] = jnp.where(lane >= sub, both, 0.0) * (1.0 / 256.0)
    lower = jnp.where(lane < sub, both, jnp.where(lane == sub, 1.0 / both, 0.0))
    lh, ll = split(lower)
    th, tl = split(lower.T)
    to_coupling = jnp.concatenate([lh, ll, lh], axis=1)
    to_weights = jnp.concatenate([th, tl, th], axis=1)
    copies = []
    for n in range(COLS // TILE):
        columns = pl.ds(n * TILE, TILE)
        wh, wl = split(total[:, columns])
        c = plain(to_coupling, jnp.concatenate([wh, wh, wl], axis=0))
        coupling[:, columns] = c
        ch, cl = split(c)
        xh, xl = split(plain(to_weights, jnp.concatenate([ch, ch, cl], axis=0)))
        x2[:, columns] = jnp.concatenate([xh, xh, xl], axis=0)
        for block in range(BLOCKS):
            rows = pl.ds(block * BLOCK, BLOCK)
            p = panel2[rows]
            left = jnp.concatenate([p, p[:, :PANEL]], axis=1)
            out[rows, columns] = kept[rows, columns] - plain(left, x2[:, columns])
            copy = pltpu.make_async_copy(
                out.at[rows, columns], updated.at[rows, columns], sems.at[n * BLOCKS + block]
            )
            copy.start()
            copies.append(copy)
    for copy in copies:
        copy.wait()


def body(snapshots):
    dma = pltpu.SemaphoreType.DMA
    snapshots = pltpu.with_memory_space_constraint(snapshots, pltpu.HBM)
    kept, panel2, total, packed = pl.pallas_call(
        gather_kernel,
        name="panel_sums",
        out_shape=[
            pltpu.VMEM((ROWS, COLS), F32),
            pltpu.VMEM((ROWS, 2 * PANEL), BF16),
            pltpu.VMEM((PANEL, COLS), F32),
            pltpu.VMEM((PANEL, PANEL), F32),
        ],
        in_specs=[pl.BlockSpec(memory_space=pltpu.HBM)],
        out_specs=[pl.BlockSpec(memory_space=pltpu.VMEM)] * 4,
        scratch_shapes=[
            pltpu.VMEM((ROWS, PANEL), F32),
            pltpu.VMEM((ROWS, COLS), BF16),
            pltpu.VMEM((ROWS, COLS), BF16),
            pltpu.VMEM((PANEL, COLS), F32),
            pltpu.VMEM((PANEL, HALF), F32),
            pltpu.VMEM((PANEL, HALF), F32),
            pltpu.VMEM((CHIPS, PIECE, HALF), F32),
            pltpu.VMEM((PANEL, PANEL), F32),
            pltpu.VMEM((CHIPS, PIECE, PANEL), F32),
            pltpu.VMEM((PIECE, PANEL), F32),
            pltpu.VMEM((PIECE, PANEL), F32),
            pltpu.VMEM((PANEL, PANEL), F32),
            dma((BLOCKS,)), dma, dma((2 * CHUNKS,)), dma((CHUNKS,)), dma, dma,
            dma((CHIPS,)), dma((CHIPS,)), dma((CHIPS,)), dma((CHIPS,)), dma((CHIPS,)), dma((CHIPS,)),
            dma((CHIPS,)), dma((CHIPS,)), dma, dma, dma((CHIPS,)), dma((CHIPS,)), dma((4,)), dma,
            pltpu.SemaphoreType.REGULAR((3,)),
        ],
        compiler_params=pltpu.CompilerParams(
            collective_id=0, has_side_effects=True, vmem_limit_bytes=24 << 20
        ),
    )(snapshots)
    kept, panel2, total, packed = [
        pltpu.with_memory_space_constraint(a, pltpu.VMEM) for a in (kept, panel2, total, packed)
    ]
    return pl.pallas_call(
        apply_kernel,
        name="apply",
        out_shape=[
            jax.ShapeDtypeStruct((PANEL, PANEL), F32),
            jax.ShapeDtypeStruct((PANEL, COLS), F32),
            jax.ShapeDtypeStruct((ROWS, COLS), F32),
        ],
        in_specs=[pl.BlockSpec(memory_space=pltpu.VMEM)] * 4,
        out_specs=[
            pl.BlockSpec(memory_space=pltpu.VMEM),
            pl.BlockSpec(memory_space=pltpu.VMEM),
            pl.BlockSpec(memory_space=pl.ANY),
        ],
        scratch_shapes=[
            pltpu.VMEM((ROWS, COLS), F32),
            pltpu.VMEM((3 * PANEL, COLS), BF16),
            dma((BLOCKS * COLS // TILE,)),
        ],
        compiler_params=pltpu.CompilerParams(vmem_limit_bytes=24 << 20),
    )(kept, panel2, total, packed)


def solution(mesh):
    in_specs = (P("rows", "cols"),)
    out_specs = (P(), P(None, "cols"), P("rows", "cols"))
    return jax.shard_map(body, mesh=mesh, in_specs=in_specs, out_specs=out_specs, check_vma=False)
```

profile of v0, /device:TPU:3, one launch (start us, length us, event | category | flops | bytes accessed | tf_op | source)
XLA Modules:
  0.0 48.7 jit_solution(17564737556476968098)
XLA Ops:
  0.6 42.9 %panel_sums.1 = (f32[2048,1024]{1,0:T(8,128)S(1)}, bf16[2048,256]{1,0:T(8,128)(2,1)S(1)}, f32[128,1024]{1,0:T(8,128)S(1)}, f32[128,128]{1,0:T(8,128)S(1)}) custom-call(f32[2048,1024]{1,0:T(8,128)} %snap.1), custom_call_target="tpu_custom_call" | custom-call | tf_op jit(solution)/shard_map/panel_sums/pallas_call | solution.py:518
  43.6 5.1 %apply.1 = (f32[128,128]{1,0:T(8,128)}, f32[128,1024]{1,0:T(8,128)}, f32[2048,1024]{1,0:T(8,128)}) custom-call(f32[2048,1024]{1,0:T(8,128)S(1)} %get-tuple-element.7.kept, bf16[2048,256]{1,0:T(8,128)(2,1)S(1)} %get-tuple-element.8.panel2, f32[128,1024]{1,0:T(8,128)S(1)} %get-tuple-element.9.total, f32[128,128]{1,0:T(8,128)S(1)} %get-tuple-element.10.packed), custom_call_target="tpu_custom_call" | custom-call | tf_op jit(solution)/shard_map/apply/pallas_call | solution.py:554
where the time goes:
time: 48.8 us; the launch traced here: 48.7 us
  Pallas kernels  48 us (98%)
  between operations  0.64 us (1%)
    pallas_call x1, Pallas kernels, body(): pl.pallas_call(gather_kernel, name='panel_sums', out_shape=[pltpu.VMEM((R...  42.9 us
    pallas_call x1, Pallas kernels, body(): pl.pallas_call(apply_kernel, name='apply', out_shape=[jax.ShapeDtypeStruc...  5.12 us

commit v1 on v0

--- a/solution.py
+++ b/solution.py
@@ -17,8 +17,11 @@
 BLOCKS = ROWS // BLOCK
 CHUNK = 64
 CHUNKS = ROWS // CHUNK
-SIDE = CHUNKS // 2
-DIRECT = 3
+RIGHT = 16
+LEFT = CHUNKS - RIGHT
+HEAD = RIGHT - LEFT
+RIGHT_DIRECT = 6
+LEFT_DIRECT = 8
 PER = BLOCK // CHUNK
 PIECE = PANEL // CHIPS
 TILE = 512
@@ -175,24 +178,29 @@
     def first(chunk, target, extra=0):
         rows = chunk_rows(chunk)
         return pltpu.make_async_remote_copy(
-            src_ref=snap.at[rows, pl.ds(0, PANEL)], dst_ref=pbuf.at[rows], send_sem=bs_send.at[chunk + extra],
+            src_ref=pbuf.at[rows], dst_ref=pbuf.at[rows], send_sem=bs_send.at[chunk + extra],
             recv_sem=bs_recv.at[chunk], device_id=(row, target), device_id_type=MESH,
         )
 
     @pl.when(col == 0)
     def _():
+        def send_right(step, carry):
+            first(step, 1).start()
+            return carry
+
         def send(step, carry):
-            first(step, 1).start()
-            first(step + SIDE, 3).start()
-            return carry
-
-        def send_direct(step, carry):
-            first(step + SIDE, 1, CHUNKS).start()
-            first(step, 3, CHUNKS).start()
-            return carry
-
-        lax.fori_loop(0, SIDE, send, 0)
-        lax.fori_loop(SIDE - DIRECT, SIDE, send_direct, 0)
+            first(step + HEAD, 1).start()
+            first(step + RIGHT, 3).start()
+            return carry
+
+        panel_load.wait()
+        lax.fori_loop(0, HEAD, send_right, 0)
+        lax.fori_loop(0, LEFT, send, 0)
+        for step in range(max(RIGHT_DIRECT, LEFT_DIRECT)):
+            if step < LEFT_DIRECT:
+                first(CHUNKS - LEFT_DIRECT + step, 1, CHUNKS).start()
+            if step < RIGHT_DIRECT:
+                first(RIGHT - RIGHT_DIRECT + step, 3, CHUNKS).start()
         lax.fori_loop(0, BLOCKS, start_load, 0)
         announce(0)
 
@@ -238,7 +246,6 @@
 
     @pl.when(col == 0)
     def _():
-        panel_load.wait()
 
         def one(block, carry):
             widen(block * BLOCK, BLOCK)
@@ -271,19 +278,25 @@
 
     @pl.when(col != 0)
     def _():
+        def ordered(step, right, head, count):
+            turn = jnp.maximum(step - head, 0)
+            both_ways = jnp.where(step < head, step, jnp.where(turn % 2 == 0, head, right) + turn // 2)
+            straight = (step + jnp.where(col == 3, right, 0)) % count
+            return jnp.where(col == 2, both_ways, straight)
+
         def pass_on(step):
-            straight = (step + jnp.where(col == 3, SIDE, 0)) % CHUNKS
-            chunk = jnp.where(col == 2, (step % 2) * SIDE + step // 2, straight)
-            onward = jnp.where(chunk < SIDE, col + 1, col - 1)
+            chunk = ordered(step, RIGHT, HEAD, CHUNKS)
+            onward = jnp.where(chunk < RIGHT, col + 1, col - 1)
+            shared = jnp.where(chunk < RIGHT, RIGHT - RIGHT_DIRECT, CHUNKS - LEFT_DIRECT)
+            limit = jnp.where(col == 2, shared, CHUNKS)
             relay(chunk, 0).wait_recv()
 
-            @pl.when((onward > 0) & (onward < 4) & ((col != 2) | (chunk % SIDE < SIDE - DIRECT)))
+            @pl.when((onward > 0) & (onward < 4) & (chunk < limit))
             def _():
                 relay(chunk, onward).start()
 
         def work(index):
-            straight = (index + jnp.where(col == 3, UNITS // 2, 0)) % UNITS
-            unit = jnp.where(col == 2, (index % 2) * (UNITS // 2) + index // 2, straight)
+            unit = ordered(index, RIGHT // 2, HEAD // 2, UNITS)
             widen(unit * UNIT, UNIT)
             accumulate(unit * UNIT, UNIT)
 
@@ -304,6 +317,7 @@
             return carry
 
         announce(0)
+
         lax.fori_loop(0, 2, early, 0)
         await_round(0)
         announce(1)
@@ -376,6 +390,23 @@
         scatter(at).start()
     parts[chip] = mine[pl.ds(pl.multiple_of(chip * PIECE, PIECE), PIECE)]
 
+    def sent_on(chunk, carry):
+        relay(chunk, 0).wait_send()
+        return carry
+
+    @pl.when(col == 1)
+    def _():
+        lax.fori_loop(0, RIGHT, sent_on, 0)
+
+    @pl.when(col == 2)
+    def _():
+        lax.fori_loop(0, RIGHT - RIGHT_DIRECT, sent_on, 0)
+        lax.fori_loop(RIGHT, CHUNKS - LEFT_DIRECT, sent_on, 0)
+
+    @pl.when(col == 3)
+    def _():
+        lax.fori_loop(RIGHT, CHUNKS, sent_on, 0)
+
     def send_packed(target):
         return pltpu.make_async_remote_copy(
             src_ref=packed, dst_ref=packed, send_sem=u_send.at[target], recv_sem=u_recv,
@@ -390,6 +421,17 @@
         for target in (2, 1, 3):
             send_packed(target).start()
 
+        def sent(chunk, carry):
+            first(chunk, 1).wait_send()
+            return carry
+
+        lax.fori_loop(0, CHUNKS, sent, 0)
+
+        for step in range(LEFT_DIRECT):
+            first(CHUNKS - LEFT_DIRECT + step, 1, CHUNKS).wait_send()
+        for step in range(RIGHT_DIRECT):
+            first(RIGHT - RIGHT_DIRECT + step, 3, CHUNKS).wait_send()
+
     for at in NEAR:
         scattered(at).wait_recv()
     half = pl.ds(pl.multiple_of(core * HALF, HALF), HALF)
@@ -421,12 +463,13 @@
         gather(at).start()
     onward(chip, half).start()
     for at in NEAR:
+        scatter(at).wait_send()
+    for at in NEAR:
         gathered(at).wait_recv()
         onward(away(at), half).start()
     other_half = pl.ds(pl.multiple_of((1 - core) * HALF, HALF), HALF)
 
     for at in NEAR:
-        scatter(at).wait_send()
         gather(at).wait_send()
 
     @pl.when(col == 0)
@@ -436,36 +479,6 @@
             gram_gather(at).wait_send()
         for target in (2, 1, 3):
             send_packed(target).wait_send()
-
-        def sent(chunk, carry):
-            first(chunk, 1).wait_send()
-            return carry
-
-        lax.fori_loop(0, CHUNKS, sent, 0)
-
-        def sent_direct(step, carry):
-            first(step + SIDE, 1, CHUNKS).wait_send()
-            first(step, 3, CHUNKS).wait_send()
-            return carry
-
-        lax.fori_loop(SIDE - DIRECT, SIDE, sent_direct, 0)
-
-    def sent_on(chunk, carry):
-        relay(chunk, 0).wait_send()
-        return carry
-
-    @pl.when(col == 1)
-    def _():
-        lax.fori_loop(0, SIDE, sent_on, 0)
-
-    @pl.when(col == 2)
-    def _():
-        lax.fori_loop(0, SIDE - DIRECT, sent_on, 0)
-        lax.fori_loop(SIDE, CHUNKS - DIRECT, sent_on, 0)
-
-    @pl.when(col == 3)
-    def _():
-        lax.fori_loop(SIDE, CHUNKS, sent_on, 0)
 
     @pl.when(col != 0)
     def _():

time: 48.8 us -> 47.2 us (0.967)
  Pallas kernels: 48 us -> 46.4 us
    pallas_call x1, Pallas kernels: 42.9 us -> 41.3 us  [body(): pl.pallas_call(gather_kernel, name='panel_sums', out_shape=[pltpu.VMEM((R...]
where the time goes in v1:
time: 47.2 us; the launch traced here: 47.1 us
  Pallas kernels  46.4 us (98%)
  between operations  0.64 us (1%)
    pallas_call x1, Pallas kernels, body(): pl.pallas_call(gather_kernel, name='panel_sums', out_shape=[pltpu.VMEM((R...  41.3 us
    pallas_call x1, Pallas kernels, body(): pl.pallas_call(apply_kernel, name='apply', out_shape=[jax.ShapeDtypeStruc...  5.12 us

profile of v1, /device:TPU:3, one launch (start us, length us, event | category | flops | bytes accessed | tf_op | source)
XLA Modules:
  0.0 47.1 jit_solution(9433956502118615195)
XLA Ops:
  0.6 41.3 %panel_sums.1 = (f32[2048,1024]{1,0:T(8,128)S(1)}, bf16[2048,256]{1,0:T(8,128)(2,1)S(1)}, f32[128,1024]{1,0:T(8,128)S(1)}, f32[128,128]{1,0:T(8,128)S(1)}) custom-call(f32[2048,1024]{1,0:T(8,128)} %snap.1), custom_call_target="tpu_custom_call" | custom-call | tf_op jit(solution)/shard_map/panel_sums/pallas_call | solution.py:531
  41.9 5.1 %apply.1 = (f32[128,128]{1,0:T(8,128)}, f32[128,1024]{1,0:T(8,128)}, f32[2048,1024]{1,0:T(8,128)}) custom-call(f32[2048,1024]{1,0:T(8,128)S(1)} %get-tuple-element.7.kept, bf16[2048,256]{1,0:T(8,128)(2,1)S(1)} %get-tuple-element.8.panel2, f32[128,1024]{1,0:T(8,128)S(1)} %get-tuple-element.9.total, f32[128,128]{1,0:T(8,128)S(1)} %get-tuple-element.10.packed), custom_call_target="tpu_custom_call" | custom-call | tf_op jit(solution)/shard_map/apply/pallas_call | solution.py:567
